TPU v7x, 32 devices: a whole 2x2x4 slice. The times are simulated.
32 devices in a mesh: dp: 2 (over x), ctx: 4 (over y, core), uly: 4 (over z).
Axes of the slice: x: 2, y: 2, z: 4, core: 2. Of those that a mesh axis runs over, the one named last changes fastest.
Arguments:
- queries: bfloat16 [2, 3072, 1536], P('dp', ('ctx', 'uly')), may hold values from -4.5 to 4.5
- key_rows: bfloat16 [2, 3072, 1536], P('dp', ('ctx', 'uly')), may hold values from -4.5 to 4.5
- value_rows: bfloat16 [2, 3072, 1536], P('dp', ('ctx', 'uly')), may hold values from -5 to 5
- out_grad: bfloat16 [2, 3072, 3072], P('dp', 'ctx'), may hold values from -6 to 6
- out_weight: bfloat16 [1536, 3072], P('uly'), may hold values from -0.15625 to 0.15625
- tile_lists: int32 [8, 6], replicated, may hold values from -1 to 7, as said below
- windows: int32 [12, 2], replicated, may hold values from 0 to 1, as said below
Outputs:
- query_grad: bfloat16 [2, 3072, 1536], P('dp', ('ctx', 'uly'))
- key_grad: bfloat16 [2, 3072, 1536], P('dp', ('ctx', 'uly'))
- value_grad: bfloat16 [2, 3072, 1536], P('dp', ('ctx', 'uly'))
- weight_grad: bfloat16 [1536, 3072], P('uly')
Inputs may be any that keep to these rules, and one draw needn't show every extreme that they name: `tile_lists`: entry j of row Q = f * 2 + s is -1 or (f + j // 2 - 1) * 2 + j % 2; it is -1 wherever f + j // 2 - 1 lies outside 0 to 3, and never at an in-range entry with j % 2 == s. Of any two consecutive heads, at least one has windows[h, 0] = 1.
All inputs are finite; a program needn't handle non-finite values.
Results may differ from a plain program's by a relative error of at most 0.014.
Values may be sent and summed in bfloat16 or wider, within the bound.
A program may use at most 192 MiB of HBM per device.

v0:
```python
import jax
import jax.numpy as jnp
from jax import lax
from jax.sharding import PartitionSpec as P

HEADS = 12
HD = 128
TILE = 384
TW = 2
FT_DEV = 1


def extended(x, sides, width):
    for axis, dim in sides:
        count, length = (lax.axis_size(axis), x.shape[dim])
        up = [(i, (i + 1) % count) for i in range(count - 1)]
        down = [(j, i) for i, j in up]
        last = lax.slice_in_dim(x, length - width, length, axis=dim)
        initial = lax.slice_in_dim(x, 0, width, axis=dim)
        before = lax.ppermute(last, axis, up)
        after = lax.ppermute(initial, axis, down)
        x = jnp.concatenate([before, x, after], axis=dim)
    return x


def cross_rounded(parts):
    lowered = lax.optimization_barrier(parts.astype(jnp.bfloat16)).astype(jnp.float32)
    return jnp.concatenate([lowered[0:1], parts[1:2], lowered[2:3]], axis=0)


def score_grid_of(query_tile, key_window):
    scaling = HD ** (-0.5)
    scores = jnp.dot(query_tile, key_window.T, preferred_element_type=jnp.float32) * scaling
    return scores.reshape(TW, TILE, 3 * TW, TILE)


def forward_block(query_tile, key_window, value_window, allow):
    score_grid = score_grid_of(query_tile, key_window)
    key_mask = allow[:, None, :, None]
    row_max = jnp.max(jnp.where(key_mask, score_grid, -jnp.inf), axis=(2, 3), keepdims=True)
    raised = jnp.where(key_mask, jnp.exp(score_grid - row_max), 0.0)
    totals = jnp.sum(raised, axis=(2, 3), keepdims=True)
    mixing = (raised / totals).reshape(TW * TILE, 3 * TW * TILE)
    out_low = jnp.dot(
        mixing.astype(jnp.bfloat16), value_window, preferred_element_type=jnp.float32
    ).astype(jnp.bfloat16)
    return (mixing, out_low, row_max, totals)


def backward_block(query_tile, key_window, value_window, grad_tile, mixing, out_low):
    scaling = HD ** (-0.5)
    mixing_low = mixing.astype(jnp.bfloat16)
    row_delta = jnp.sum(
        out_low.astype(jnp.float32) * grad_tile.astype(jnp.float32), axis=1, keepdims=True
    )
    value_part = lax.dot_general(
        mixing_low, grad_tile, (((0,), (0,)), ((), ())), preferred_element_type=jnp.float32
    )
    prob_grad = jnp.dot(grad_tile, value_window.T, preferred_element_type=jnp.float32)
    score_grad = (mixing * (prob_grad - row_delta) * scaling).astype(jnp.bfloat16)
    query_part = jnp.dot(score_grad, key_window, preferred_element_type=jnp.float32)
    key_part = lax.dot_general(
        score_grad, query_tile, (((0,), (0,)), ((), ())), preferred_element_type=jnp.float32
    )
    return (query_part, key_part, value_part)


def weight_sum(attended, token_grads):
    local_term = lax.dot_general(
        attended, token_grads, (((0,), (0,)), ((), ())), preferred_element_type=jnp.float32
    )
    grand_total = lax.psum(local_term, ("dp", "ctx"))
    return (grand_total / lax.axis_size("dp")).astype(jnp.bfloat16)


def on_device(queries, key_rows, value_rows, out_grad, out_weight, tile_lists, windows):
    heads_here = HEADS // lax.axis_size("uly")
    width_here = heads_here * HD
    layer_rows = TW * TILE
    span_rows = FT_DEV * layer_rows
    query_heads, pair_heads = (
        lax.all_to_all(queries[None], "uly", split_axis=3, concat_axis=2, tiled=True),
        lax.all_to_all(
            jnp.stack([key_rows, value_rows]), "uly", split_axis=3, concat_axis=2, tiled=True
        ),
    )
    query_heads = query_heads.reshape(FT_DEV, layer_rows, heads_here, HD)
    window = extended(pair_heads, (("ctx", 1),), 1)
    window = window.reshape(2, FT_DEV + 2, layer_rows, heads_here, HD)
    grad_out = lax.dot_general(
        out_grad[0], out_weight, (((1,), (1,)), ((), ())), preferred_element_type=jnp.float32
    )
    grad_out = grad_out.astype(jnp.bfloat16).reshape(FT_DEV, layer_rows, heads_here, HD)
    ctx_at = lax.axis_index("ctx")
    uly_at = lax.axis_index("uly")
    list_rows = lax.dynamic_slice_in_dim(tile_lists, ctx_at * (FT_DEV * TW), FT_DEV * TW, 0)
    listed = (list_rows >= 0).reshape(FT_DEV, TW, 3 * TW)
    reach_rows = lax.dynamic_slice_in_dim(windows, uly_at * heads_here, heads_here, 0)
    slot_ids = jnp.arange(3 * TW, dtype=jnp.int32)
    slot_time = slot_ids // TW - 1
    slot_space = slot_ids % TW
    spot_ids = jnp.arange(TW, dtype=jnp.int32)
    near_time = jnp.abs(slot_time)[None, :] <= reach_rows[:, 0:1]
    near_space = (
        jnp.abs(slot_space[None, :] - spot_ids[:, None])[None, :, :]
        <= reach_rows[:, 1][:, None, None]
    )
    allowed = listed[:, None, :, :] & near_time[None, :, None, :] & near_space[None, :, :, :]

    def tiles_of(frame_at, head_at):
        query_tile = query_heads[frame_at, :, head_at]
        key_window = window[0, frame_at : frame_at + 3, :, head_at].reshape(3 * layer_rows, HD)
        value_window = window[1, frame_at : frame_at + 3, :, head_at].reshape(3 * layer_rows, HD)
        return (query_tile, key_window, value_window)

    def assemble(per_block):
        frames_list = [jnp.stack(per_block[0], axis=1)]
        return jnp.stack(frames_list, axis=0).reshape(span_rows, width_here)

    pair_total = jnp.zeros((2, FT_DEV + 2, layer_rows, heads_here, HD), jnp.float32)
    out_blocks = [[None] * heads_here]
    query_blocks = [[None] * heads_here]

    def add_back(pair_total, frame_at, head_at, mixing, out_low):
        query_tile, key_window, value_window = tiles_of(frame_at, head_at)
        query_part, key_part, value_part = backward_block(
            query_tile, key_window, value_window, grad_out[frame_at, :, head_at], mixing, out_low
        )
        query_blocks[frame_at][head_at] = query_part.astype(jnp.bfloat16)
        pair_total = pair_total.at[0, frame_at : frame_at + 3, :, head_at].add(
            cross_rounded(key_part.reshape(3, layer_rows, HD))
        )
        pair_total = pair_total.at[1, frame_at : frame_at + 3, :, head_at].add(
            cross_rounded(value_part.reshape(3, layer_rows, HD))
        )
        return pair_total

    frame_at = 0
    for head_at in range(heads_here):
        query_tile, key_window, value_window = tiles_of(frame_at, head_at)
        mixing, out_low, row_max, totals = forward_block(
            query_tile, key_window, value_window, allowed[frame_at, head_at]
        )
        out_blocks[frame_at][head_at] = out_low
        pair_total = add_back(pair_total, frame_at, head_at, mixing, out_low)
    attended = assemble(out_blocks)
    weight_grad = weight_sum(attended, out_grad[0])
    outgoing = jnp.stack([pair_total[:, 0], pair_total[:, FT_DEV + 1]]).astype(jnp.bfloat16)
    returned = extended(outgoing, (("ctx", 0),), 1).astype(jnp.float32)
    own_grads = pair_total[:, 1 : FT_DEV + 1]
    own_grads = own_grads.at[:, 0].add(returned[0])
    own_grads = own_grads.at[:, FT_DEV - 1].add(returned[3])
    key_heads = own_grads[0].reshape(1, span_rows, width_here).astype(jnp.bfloat16)
    value_heads = own_grads[1].reshape(1, span_rows, width_here).astype(jnp.bfloat16)
    query_grad_heads = assemble(query_blocks).reshape(1, span_rows, width_here)
    tokens_back = (
        lax.all_to_all(query_grad_heads, "uly", split_axis=1, concat_axis=2, tiled=True),
        lax.all_to_all(key_heads, "uly", split_axis=1, concat_axis=2, tiled=True),
        lax.all_to_all(value_heads, "uly", split_axis=1, concat_axis=2, tiled=True),
    )
    return (tokens_back[0], tokens_back[1], tokens_back[2], weight_grad)


def solution(mesh):
    in_specs = (
        P("dp", ("ctx", "uly"), None),
        P("dp", ("ctx", "uly"), None),
        P("dp", ("ctx", "uly"), None),
        P("dp", "ctx", None),
        P("uly", None),
        P(),
        P(),
    )
    out_specs = (
        P("dp", ("ctx", "uly"), None),
        P("dp", ("ctx", "uly"), None),
        P("dp", ("ctx", "uly"), None),
        P("uly", None),
    )
    return jax.shard_map(
        on_device, mesh=mesh, in_specs=in_specs, out_specs=out_specs, check_vma=False
    )
```

profile of v0, /device:TPU:0, one launch (start us, length us, event | category | flops | bytes accessed | tf_op | source)
XLA Modules:
  0.0 331.9 jit_solution(7752519671233475620)
XLA Ops:
  7.2 1.5 pad_maximum_fusion.4
  8.7 2.9 copy.189
  11.5 6.4 %all-to-all-start = ((bf16[2,1,192,1536]{2,0,1,3:T(2,128)(2,1)}), bf16[2,1,192,1536]{2,0,1,3:T(2,128)(2,1)}, u32[]{:S(2)}, u32[]{:S(2)}) async-start(bf16[2,1,192,1536]{2,0,1,3:T(2,128)(2,1)} %copy.189), calls=%async_computation | async-start | bytes 3145728 | tf_op jit(solution)/shard_map/all_to_all | solution.py:83
  18.0 2.8 copy.197
  21.4 9.9 %reduce.34 = bf16[1536,192]{1,0:T(8,128)(2,1)S(1)} reduce(bf16[1536,1,1,192]{3,2,1,0:T(2,128)(2,1)} %bitcast.300, bf16[]{:T(256)} %broadcast.396), dimensions={1,2}, to_apply=%bitcast.238.reduce_sub_computation | reduce | bytes 1179650
  31.3 1.7 reshape.571
  34.0 21.1 %all-to-all-done = bf16[2,1,192,1536]{2,0,1,3:T(2,128)(2,1)} async-done(((bf16[2,1,192,1536]{2,0,1,3:T(2,128)(2,1)}), bf16[2,1,192,1536]{2,0,1,3:T(2,128)(2,1)}, u32[]{:S(2)}, u32[]{:S(2)}) %all-to-all-start) | async-done | bytes 1179680 | tf_op jit(solution)/shard_map/all_to_all | solution.py:83
  55.1 4.2 %all-to-all-start.1 = ((bf16[4,2,36864]{2,1,0:T(2,128)(2,1)}), bf16[4,2,36864]{2,1,0:T(2,128)(2,1)}, u32[]{:S(2)}, u32[]{:S(2)}) async-start(bf16[4,2,36864]{2,1,0:T(2,128)(2,1)} %reshape.571), calls=%async_computation.1 | async-start | bytes 1179648 | tf_op jit(solution)/shard_map/all_to_all | solution.py:82
  59.2 4.3 %copy.237 = bf16[2,1,192,4,384]{4,3,2,0,1:T(4,128)(2,1)S(1)} copy(bf16[2,1,192,4,384]{2,0,4,3,1:T(2,128)(2,1)} %bitcast.5) | data formatting | bytes 2359296 | tf_op jit(solution)/shard_map/all_to_all | solution.py:83
  66.1 4.2 %collective-permute-start = (bf16[2,1,768,384]{3,2,0,1:T(8,128)(2,1)}, bf16[2,1,768,384]{3,2,0,1:T(8,128)(2,1)}, u32[]{:S(2)}, u32[]{:S(2)}) collective-permute-start(bf16[2,1,768,384]{3,2,0,1:T(8,128)(2,1)} %bitcast.7), channel_id=1, source_target_pairs={{0,4},{4,8},{8,12},{1,5},{5,9},{9,13},{2,6},{6,10},{10,14},{3,7},{... | collective-permute-start | bytes 3538952 | tf_op jit(solution)/shard_map/ppermute | solution.py:20
  72.5 3.2 copy.206
  77.3 3.2 copy.211
  82.1 3.2 copy.201
  88.6 5.4 %fusion.34 = bf16[768,384]{0,1:T(8,128)(2,1)} fusion(bf16[384,3072]{1,0:T(8,128)(2,1)S(1)} %copy-done, bf16[1,768,3072]{2,1,0:T(8,128)(2,1)} %param.26), kind=kOutput, calls=%fused_computation.50 | convolution fusion | flops 1812234240 | bytes 7667712 | tf_op jit(solution)/shard_map/dot_general | solution.py:90
  94.1 2.6 reshape.572
  98.1 1.8 fusion.83
  99.9 2.6 copy.292
  102.5 1.4 reshape.570
  104.0 1.6 copy.194
  105.6 1.6 copy.192
  107.6 1.5 fusion.81
  109.1 1.5 copy.204
  113.0 2.1 copy.207
  117.6 2.5 fusion.6
  120.1 1.9 fusion.14
  122.1 3.9 %fusion.92 = (bf16[2304,128]{0,1:T(8,128)(2,1)}, f32[2304,128]{0,1:T(8,128)}) fusion(bf16[1,768,3,128]{1,3,2,0:T(8,128)(2,1)S(1)} %bitcast.351, f32[768]{0:T(1024)S(1)} %fusion.14, pred[768,2304]{0,1:T(32,128)(4,1)S(1)} %copy-done.6, f32[768]{0:T(1024)S(1)} %get-tuple-element.137, f32[2304,768]{1,0:T(8,128)S(1)} %get-tuple-element.138), kind=kOutput, calls=%fused_computation.143 | convolution fusion | flops 462127104 | bytes 10821632 | tf_op jit(solution)/shard_map/dot_general | solution.py:56
  127.4 1.8 fusion.18
  129.2 3.4 %fusion.96 = (bf16[2304,128]{0,1:T(8,128)(2,1)}, f32[2304,128]{0,1:T(8,128)}) fusion(bf16[1,768,3,128]{1,3,2,0:T(8,128)(2,1)S(1)} %bitcast.352, f32[768]{0:T(1024)S(1)} %fusion.18, pred[768,2304]{0,1:T(32,128)(4,1)S(1)} %copy-done.8, f32[768]{0:T(1024)S(1)} %get-tuple-element.139, f32[2304,768]{1,0:T(8,128)S(1)} %get-tuple-element.140), kind=kOutput, calls=%fused_computation.147 | convolution fusion | flops 462127104 | bytes 10821632 | tf_op jit(solution)/shard_map/dot_general | solution.py:56
  132.7 2.5 fusion.48
  136.6 1.9 fusion.16
  138.6 2.6 fusion.45
  141.2 3.8 %multiply_reduce_fusion.2 = (f32[768]{0:T(1024)}, f32[768]{0:T(1024)S(1)}, f32[768]{0:T(1024)}, bf16[768,128]{0,1:T(8,128)(2,1)}) fusion(bf16[1,768,3,128]{1,3,2,0:T(8,128)(2,1)S(1)} %bitcast.353, bf16[768,128]{0,1:T(8,128)(2,1)S(1)} %fusion.48, bf16[768,128]{0,1:T(8,128)(2,1)S(1)} %fusion.45, bf16[2304,128]{1,0:T(8,128)(2,1)S(1)} %bitcast.334, ...), kind=kOutput, calls=%fused_computation.89 | convolution fusion | flops 463107840 | bytes 10632192 | tf_op jit(solution)/shard_map/dot_general | solution.py:44
  145.0 3.1 multiply_convert_fusion
  148.2 1.4 fusion.53
  149.6 2.6 fusion.95
  152.2 3.5 %fusion.94 = (bf16[2304,128]{0,1:T(8,128)(2,1)}, f32[2304,128]{0,1:T(8,128)}) fusion(bf16[1,768,3,128]{1,3,2,0:T(8,128)(2,1)S(1)} %bitcast.355, f32[768]{0:T(1024)S(1)} %fusion.16, pred[768,2304]{0,1:T(32,128)(4,1)S(1)} %copy-done.5, f32[768]{0:T(1024)S(1)} %get-tuple-element.141, f32[2304,768]{1,0:T(8,128)S(1)} %get-tuple-element.142), kind=kOutput, calls=%fused_computation.145 | convolution fusion | flops 462127104 | bytes 10821632 | tf_op jit(solution)/shard_map/dot_general | solution.py:56
  157.2 1.8 slice_bitcast_fusion.7
  161.5 1.8 slice_bitcast_fusion.3
  163.3 6.6 %multiply_convert_fusion.2 = bf16[768,2304]{0,1:T(8,128)(2,1)S(1)} fusion(bf16[2304,128]{1,0:T(8,128)(2,1)} %bitcast.333, f32[768]{0:T(1024)} %get-tuple-element.100, bf16[1,768,3,128]{1,3,2,0:T(8,128)(2,1)} %bitcast.349, f32[768]{0:T(1024)S(1)} %fusion.14, pred[768,2304]{0,1:T(32,128)(4,1)} %copy.201, f32[768]{0:T(1024)S(1)} %get-tuple-element.137, ...), kind=kOutput, calls=%fused_computation.17 | convolution fusion | flops 467140608 | bytes 13182976 | tf_op jit(solution)/shard_map/dot_general | solution.py:59
  169.9 1.9 copy-done.11
  171.8 2.3 fusion.91
  174.7 2.1 copy.224
  180.0 1.8 slice_bitcast_fusion.4
  181.8 1.8 slice_bitcast_fusion.8
  183.6 5.1 %multiply_convert_fusion.1 = bf16[768,2304]{0,1:T(8,128)(2,1)S(1)} fusion(bf16[2304,128]{1,0:T(8,128)(2,1)S(1)} %bitcast.332, f32[768]{0:T(1024)S(1)} %copy-done.46, bf16[1,768,3,128]{1,3,2,0:T(8,128)(2,1)} %bitcast.350, f32[768]{0:T(1024)S(1)} %fusion.16, pred[768,2304]{0,1:T(32,128)(4,1)S(1)} %copy-done.5, f32[768]{0:T(1024)S(1)} %get-tuple-element.141, ...), kind=kOutput, calls=%fused_computation.16 | convolution fusion | flops 467140608 | bytes 13181952 | tf_op jit(solution)/shard_map/dot_general | solution.py:59
  188.7 1.9 copy-done.13
  192.5 1.4 copy.222
  196.9 1.7 fusion.37
  199.0 2.0 fusion.38
  201.8 2.4 copy-done.2
  205.4 3.3 collective-permute-start.2
  208.7 1.4 collective-permute-start.3
  212.9 4.2 %reduce.35 = bf16[768,384]{1,0:T(8,128)(2,1)S(1)} reduce(bf16[768,1,384]{2,1,0:T(2,128)(2,1)S(1)} %bitcast.312, bf16[]{:T(256)} %broadcast.396), dimensions={1}, to_apply=%bitcast.240.reduce_sub_computation | reduce | bytes 1179650
  218.1 5.0 %all-to-all-start.2 = ((bf16[4,2,36864]{2,1,0:T(2,128)(2,1)}), bf16[4,2,36864]{2,1,0:T(2,128)(2,1)S(1)}, u32[]{:S(2)}, u32[]{:S(2)}) async-start(bf16[4,2,36864]{2,1,0:T(2,128)(2,1)} %reshape.573), calls=%async_computation.2 | async-start | bytes 1179648 | tf_op jit(solution)/shard_map/all_to_all | solution.py:157
  224.3 6.4 %fusion.9 = f32[384,3072]{1,0:T(8,128)} fusion(bf16[768,384]{0,1:T(8,128)(2,1)S(1)} %bitcast.340, bf16[1,768,3072]{2,1,0:T(8,128)(2,1)} %param.26), kind=kOutput, calls=%fused_computation.18 | convolution fusion | flops 1811939328 | bytes 10027008 | tf_op jit(solution)/shard_map/dot_general | solution.py:69
  230.8 2.8 fusion.21
  235.1 4.2 %reduce.36 = bf16[768,384]{1,0:T(8,128)(2,1)S(1)} reduce(bf16[768,1,384]{2,1,0:T(2,128)(2,1)S(1)} %bitcast.313, bf16[]{:T(256)} %broadcast.396), dimensions={1}, to_apply=%bitcast.242.reduce_sub_computation | reduce | bytes 1179650
  240.4 4.9 %all-to-all-start.3 = ((bf16[4,2,36864]{2,1,0:T(2,128)(2,1)}), bf16[4,2,36864]{2,1,0:T(2,128)(2,1)S(1)}, u32[]{:S(2)}, u32[]{:S(2)}) async-start(bf16[4,2,36864]{2,1,0:T(2,128)(2,1)} %reshape.575), calls=%async_computation.3 | async-start | bytes 1179648 | tf_op jit(solution)/shard_map/all_to_all | solution.py:158
  246.6 4.2 %reduce.37 = bf16[768,384]{1,0:T(8,128)(2,1)S(1)} reduce(bf16[768,1,384]{2,1,0:T(2,128)(2,1)S(1)} %bitcast.311, bf16[]{:T(256)} %broadcast.396), dimensions={1}, to_apply=%bitcast.244.reduce_sub_computation | reduce | bytes 1179650
  251.8 10.2 %all-to-all-done.3 = bf16[4,2,36864]{2,1,0:T(2,128)(2,1)S(1)} async-done(((bf16[4,2,36864]{2,1,0:T(2,128)(2,1)}), bf16[4,2,36864]{2,1,0:T(2,128)(2,1)S(1)}, u32[]{:S(2)}, u32[]{:S(2)}) %all-to-all-start.3) | async-done | bytes 589856 | tf_op jit(solution)/shard_map/all_to_all | solution.py:158
  262.0 3.5 %all-to-all-start.4 = ((bf16[4,2,36864]{2,1,0:T(2,128)(2,1)}), bf16[4,2,36864]{2,1,0:T(2,128)(2,1)S(1)}, u32[]{:S(2)}, u32[]{:S(2)}) async-start(bf16[4,2,36864]{2,1,0:T(2,128)(2,1)} %reshape.577), calls=%async_computation.4 | async-start | bytes 1179648 | tf_op jit(solution)/shard_map/all_to_all | solution.py:159
  268.6 12.7 %all-to-all-done.4 = bf16[4,2,36864]{2,1,0:T(2,128)(2,1)S(1)} async-done(((bf16[4,2,36864]{2,1,0:T(2,128)(2,1)}), bf16[4,2,36864]{2,1,0:T(2,128)(2,1)S(1)}, u32[]{:S(2)}, u32[]{:S(2)}) %all-to-all-start.4) | async-done | bytes 589856 | tf_op jit(solution)/shard_map/all_to_all | solution.py:159
  282.9 37.6 %all-reduce.3.cloned.1.call-done = f32[384,3072]{1,0:T(8,128)} async-done(((f32[384,3072]{1,0:T(8,128)}), f32[384,3072]{1,0:T(8,128)}) %all-reduce.3.cloned.1.call-update) | async-done | bytes 4718608 | tf_op jit(solution)/shard_map/psum | solution.py:72
  320.5 4.1 %multiply_convert_fusion.3 = bf16[384,3072]{1,0:T(8,128)(2,1)} fusion(f32[384,3072]{1,0:T(8,128)} %all-reduce.3.cloned.1.call-done), kind=kLoop, calls=%fused_computation.22 | loop fusion | flops 2359296 | bytes 7077888 | tf_op jit(solution)/shard_map/convert_element_type | solution.py:73
  (181 shorter events, 51.4 us)
Async XLA Ops:
  7.2 81.5 %copy-start = (bf16[384,3072]{1,0:T(8,128)(2,1)S(1)}, bf16[384,3072]{1,0:T(8,128)(2,1)}, u32[]{:S(2)}) copy-start(bf16[384,3072]{1,0:T(8,128)(2,1)} %param.27) | copy-start | bytes 7077892
  11.5 6.5 %copy-start.36 = (bf16[1,192,1536]{2,1,0:T(8,128)(2,1)S(1)}, bf16[1,192,1536]{2,1,0:T(8,128)(2,1)}, u32[]{:S(2)}) copy-start(bf16[1,192,1536]{2,1,0:T(8,128)(2,1)} %param.23) | copy-start | bytes 1769476
  11.5 43.5 %all-to-all-start = ((bf16[2,1,192,1536]{2,0,1,3:T(2,128)(2,1)}), bf16[2,1,192,1536]{2,0,1,3:T(2,128)(2,1)}, u32[]{:S(2)}, u32[]{:S(2)}) async-start(bf16[2,1,192,1536]{2,0,1,3:T(2,128)(2,1)} %copy.189), calls=%async_computation | async-start | bytes 3145728 | tf_op jit(solution)/shard_map/all_to_all | solution.py:83
  18.0 15.7 %copy-start.42 = (s32[12,2]{0,1:T(2,128)S(1)}, s32[12,2]{0,1:T(2,128)}, u32[]{:S(2)}) copy-start(s32[12,2]{0,1:T(2,128)} %param.29) | copy-start | bytes 292
  55.1 39.0 %all-to-all-start.1 = ((bf16[4,2,36864]{2,1,0:T(2,128)(2,1)}), bf16[4,2,36864]{2,1,0:T(2,128)(2,1)}, u32[]{:S(2)}, u32[]{:S(2)}) async-start(bf16[4,2,36864]{2,1,0:T(2,128)(2,1)} %reshape.571), calls=%async_computation.1 | async-start | bytes 1179648 | tf_op jit(solution)/shard_map/all_to_all | solution.py:82
  64.8 39.2 %collective-permute-start.1 = (bf16[2,1,768,384]{3,2,0,1:T(8,128)(2,1)}, bf16[2,1,768,384]{3,2,0,1:T(8,128)(2,1)}, u32[]{:S(2)}, u32[]{:S(2)}) collective-permute-start(bf16[2,1,768,384]{3,2,0,1:T(8,128)(2,1)} %bitcast.7), channel_id=1, source_target_pairs={{4,0},{8,4},{12,8},{5,1},{9,5},{13,9},{6,2},{10,6},{14,10},{7,3},{... | collective-permute-start | bytes 3538952 | tf_op jit(solution)/shard_map/ppermute | solution.py:21
  66.1 39.5 %collective-permute-start = (bf16[2,1,768,384]{3,2,0,1:T(8,128)(2,1)}, bf16[2,1,768,384]{3,2,0,1:T(8,128)(2,1)}, u32[]{:S(2)}, u32[]{:S(2)}) collective-permute-start(bf16[2,1,768,384]{3,2,0,1:T(8,128)(2,1)} %bitcast.7), channel_id=1, source_target_pairs={{0,4},{4,8},{8,12},{1,5},{5,9},{9,13},{2,6},{6,10},{10,14},{3,7},{... | collective-permute-start | bytes 3538952 | tf_op jit(solution)/shard_map/ppermute | solution.py:20
  81.1 6.8 %copy-start.43 = (s32[5]{0:T(128)S(1)}, s32[5]{0:T(128)}, u32[]{:S(2)}) copy-start(s32[5]{0:T(128)} %constant.262.clone.1) | copy-start | bytes 64
  85.2 8.8 %copy-start.40 = (s32[2]{0:T(128)}, s32[2]{0:T(128)S(1)}, u32[]{:S(2)}) copy-start(s32[2]{0:T(128)S(1)} %iota.33) | copy-start | bytes 28
  109.1 8.5 %copy-start.6 = (pred[768,2304]{0,1:T(32,128)(4,1)S(1)}, pred[768,2304]{0,1:T(32,128)(4,1)}, u32[]{:S(2)}) copy-start(pred[768,2304]{0,1:T(32,128)(4,1)} %copy.201) | copy-start | bytes 5308420
  117.5 2.6 copy-start.9
  120.1 21.0 %copy-start.4 = (f32[2304,768]{1,0:T(8,128)}, f32[2304,768]{1,0:T(8,128)S(1)}, u32[]{:S(2)}) copy-start(f32[2304,768]{1,0:T(8,128)S(1)} %get-tuple-element.138) | copy-start | bytes 21233668
  120.1 1.9 copy-start.44
  122.1 3.9 %copy-start.8 = (pred[768,2304]{0,1:T(32,128)(4,1)S(1)}, pred[768,2304]{0,1:T(32,128)(4,1)}, u32[]{:S(2)}) copy-start(pred[768,2304]{0,1:T(32,128)(4,1)} %copy.211) | copy-start | bytes 5308420
  122.1 3.9 %copy-start.18 = (bf16[1,768,1,128]{3,2,1,0:T(2,128)(2,1)S(1)}, bf16[1,768,1,128]{3,2,1,0:T(2,128)(2,1)}, u32[]{:S(2)}) copy-start(bf16[1,768,1,128]{3,2,1,0:T(2,128)(2,1)} %get-tuple-element.116) | copy-start | bytes 589828
  129.2 3.5 %copy-start.34 = (bf16[1,3,768,1,128]{4,2,1,3,0:T(8,128)(2,1)S(1)}, bf16[1,3,768,1,128]{4,2,1,3,0:T(8,128)(2,1)}, u32[]{:S(2)}) copy-start(bf16[1,3,768,1,128]{4,2,1,3,0:T(8,128)(2,1)} %copy.212) | copy-start | bytes 1769476
  132.7 2.6 copy-start.5
  132.7 2.6 copy-start.15
  135.2 6.0 %copy-start.37 = (bf16[768,128]{0,1:T(8,128)(2,1)}, bf16[768,128]{0,1:T(8,128)(2,1)S(1)}, u32[]{:S(2)}) copy-start(bf16[768,128]{0,1:T(8,128)(2,1)S(1)} %fusion.48) | copy-start | bytes 589828
  136.6 15.6 %copy-start.3 = (f32[2304,768]{1,0:T(8,128)}, f32[2304,768]{1,0:T(8,128)S(1)}, u32[]{:S(2)}) copy-start(f32[2304,768]{1,0:T(8,128)S(1)} %get-tuple-element.142) | copy-start | bytes 21233668
  136.6 1.9 copy-start.31
  138.6 2.6 copy-start.7
  138.6 2.6 copy-start.33
  141.1 3.9 %copy-start.38 = (bf16[768,128]{0,1:T(8,128)(2,1)}, bf16[768,128]{0,1:T(8,128)(2,1)S(1)}, u32[]{:S(2)}) copy-start(bf16[768,128]{0,1:T(8,128)(2,1)S(1)} %fusion.45) | copy-start | bytes 589828
  141.2 3.9 %copy-start.45 = (bf16[768,384]{0,1:T(8,128)(2,1)S(1)}, bf16[768,384]{0,1:T(8,128)(2,1)}, u32[]{:S(2)}) copy-start(bf16[768,384]{0,1:T(8,128)(2,1)} %fusion.34) | copy-start | bytes 1769476
  152.2 3.5 %copy-start.35 = (bf16[2304,128]{0,1:T(8,128)(2,1)S(1)}, bf16[2304,128]{0,1:T(8,128)(2,1)}, u32[]{:S(2)}) copy-start(bf16[2304,128]{0,1:T(8,128)(2,1)} %get-tuple-element.146) | copy-start | bytes 1769476
  163.3 8.5 %copy-start.17 = (bf16[1,768,1,128]{3,2,1,0:T(2,128)(2,1)S(1)}, bf16[1,768,1,128]{3,2,1,0:T(2,128)(2,1)}, u32[]{:S(2)}) copy-start(bf16[1,768,1,128]{3,2,1,0:T(2,128)(2,1)} %get-tuple-element.117) | copy-start | bytes 589828
  169.9 1.9 copy-start.11
  174.7 8.9 %copy-start.46 = (f32[768]{0:T(1024)S(1)}, f32[768]{0:T(1024)}, u32[]{:S(2)}) copy-start(f32[768]{0:T(1024)} %get-tuple-element.102) | copy-start | bytes 9220
  178.1 5.4 %copy-start.32 = (bf16[1,3,768,1,128]{4,2,1,3,0:T(8,128)(2,1)S(1)}, bf16[1,3,768,1,128]{4,2,1,3,0:T(8,128)(2,1)}, u32[]{:S(2)}) copy-start(bf16[1,3,768,1,128]{4,2,1,3,0:T(8,128)(2,1)} %copy.207) | copy-start | bytes 1769476
  183.6 7.0 %copy-start.16 = (bf16[1,768,1,128]{3,2,1,0:T(2,128)(2,1)S(1)}, bf16[1,768,1,128]{3,2,1,0:T(2,128)(2,1)}, u32[]{:S(2)}) copy-start(bf16[1,768,1,128]{3,2,1,0:T(2,128)(2,1)} %get-tuple-element.115) | copy-start | bytes 589828
  188.7 1.9 copy-start.13
  194.1 1.3 copy-start.25
  194.1 1.3 copy-start.26
  194.1 1.3 copy-start.27
  195.5 1.0 copy-start.22
  195.5 1.1 copy-start.23
  195.6 1.2 copy-start.24
  195.6 1.3 copy-start.41
  196.9 2.1 copy-start.28
  196.9 2.1 copy-start.29
  196.9 2.1 copy-start.30
  198.6 2.4 copy-start.19
  198.6 2.4 copy-start.20
  198.6 2.4 copy-start.21
  201.3 2.9 copy-start.2
  204.2 5.9 %copy-start.10 = (bf16[1,3,768,1,128]{4,2,1,3,0:T(8,128)(2,1)S(1)}, bf16[1,3,768,1,128]{4,2,1,3,0:T(8,128)(2,1)}, u32[]{:S(2)}) copy-start(bf16[1,3,768,1,128]{4,2,1,3,0:T(8,128)(2,1)} %copy-done.9) | copy-start | bytes 1769476
  204.2 5.9 %copy-start.12 = (bf16[768,2304]{0,1:T(8,128)(2,1)S(1)}, bf16[768,2304]{0,1:T(8,128)(2,1)}, u32[]{:S(2)}) copy-start(bf16[768,2304]{0,1:T(8,128)(2,1)} %copy-done.11) | copy-start | bytes 10616836
  204.2 6.6 %copy-start.14 = (bf16[768,2304]{0,1:T(8,128)(2,1)S(1)}, bf16[768,2304]{0,1:T(8,128)(2,1)}, u32[]{:S(2)}) copy-start(bf16[768,2304]{0,1:T(8,128)(2,1)} %copy-done.13) | copy-start | bytes 10616836
  205.4 25.4 %collective-permute-start.2 = (bf16[1,2,768,3,128]{2,4,3,1,0:T(8,128)(2,1)S(1)}, bf16[1,2,768,3,128]{2,4,3,1,0:T(8,128)(2,1)}, u32[]{:S(2)}, u32[]{:S(2)}) collective-permute-start(bf16[1,2,768,3,128]{2,4,3,1,0:T(8,128)(2,1)S(1)} %get-tuple-element.105), channel_id=1, source_target_pairs={{0,4},{4,8},{8,12},{1,5},{5,9},{9,13},{2,6},{6,10},{10,14},{3,7},{... | collective-permute-start | bytes 3538952 | tf_op jit(solution)/shard_map/ppermute | solution.py:20
  208.7 2.9 copy-start.39
  208.7 22.1 %collective-permute-start.3 = (bf16[1,2,768,3,128]{2,4,3,1,0:T(8,128)(2,1)}, bf16[1,2,768,3,128]{2,4,3,1,0:T(8,128)(2,1)}, u32[]{:S(2)}, u32[]{:S(2)}) collective-permute-start(bf16[1,2,768,3,128]{2,4,3,1,0:T(8,128)(2,1)} %get-tuple-element.106), channel_id=1, source_target_pairs={{4,0},{8,4},{12,8},{5,1},{9,5},{13,9},{6,2},{10,6},{14,10},{7,3},{... | collective-permute-start | bytes 3538952 | tf_op jit(solution)/shard_map/ppermute | solution.py:21
  218.1 22.3 %all-to-all-start.2 = ((bf16[4,2,36864]{2,1,0:T(2,128)(2,1)}), bf16[4,2,36864]{2,1,0:T(2,128)(2,1)S(1)}, u32[]{:S(2)}, u32[]{:S(2)}) async-start(bf16[4,2,36864]{2,1,0:T(2,128)(2,1)} %reshape.573), calls=%async_computation.2 | async-start | bytes 1179648 | tf_op jit(solution)/shard_map/all_to_all | solution.py:157
  223.1 97.4 %all-reduce.3.cloned.1.call-start = ((), (), s32[]{:S(2)}) async-start(), calls=%async_computation.5 | async-start | bytes 9437184 | tf_op jit(solution)/shard_map/psum | solution.py:72
  240.4 21.6 %all-to-all-start.3 = ((bf16[4,2,36864]{2,1,0:T(2,128)(2,1)}), bf16[4,2,36864]{2,1,0:T(2,128)(2,1)S(1)}, u32[]{:S(2)}, u32[]{:S(2)}) async-start(bf16[4,2,36864]{2,1,0:T(2,128)(2,1)} %reshape.575), calls=%async_computation.3 | async-start | bytes 1179648 | tf_op jit(solution)/shard_map/all_to_all | solution.py:158
  262.0 19.3 %all-to-all-start.4 = ((bf16[4,2,36864]{2,1,0:T(2,128)(2,1)}), bf16[4,2,36864]{2,1,0:T(2,128)(2,1)S(1)}, u32[]{:S(2)}, u32[]{:S(2)}) async-start(bf16[4,2,36864]{2,1,0:T(2,128)(2,1)} %reshape.577), calls=%async_computation.4 | async-start | bytes 1179648 | tf_op jit(solution)/shard_map/all_to_all | solution.py:159
  282.0 42.6 %copy-start.1 = (bf16[384,3072]{1,0:T(8,128)(2,1)S(1)}, bf16[384,3072]{1,0:T(8,128)(2,1)}, u32[]{:S(2)}) copy-start(bf16[384,3072]{1,0:T(8,128)(2,1)} %param.27) | copy-start | bytes 7077892
Sparse Core Ops, SparseCore 0:
  230.9 89.5 all-reduce.2
where the time goes:
time: 337 us; the launch traced here: 332 us
  local copies, waits for them, and re-layouts  94.7 us (28%)
  waiting for transfers between devices  81.8 us (24%)
  matrix products  60.8 us (18%)
  other arithmetic  44.8 us (13%)
  starting transfers between devices  34.3 us (10%)
  between operations  15.5 us (5%)
    psum x1, waiting for transfers between devices, weight_sum(): grand_total = lax.psum(local_term, ('dp', 'ctx'))  37.6 us
    unnamed x4, other arithmetic  22.5 us
    all_to_all x1, waiting for transfers between devices, on_device(): lax.all_to_all(jnp.stack([key_rows, value_rows]), 'uly', split_axis=3, co...  21.1 us
    unnamed x109, local copies, waits for them, and re-layouts  19.3 us
    dot_general x3, matrix products, backward_block(): jnp.dot(grad_tile, value_window.T, preferred_element_type=jnp.float32)  14.9 us
    all_to_all x1, waiting for transfers between devices, on_device(): lax.all_to_all(value_heads, 'uly', split_axis=1, concat_axis=2, tiled=True)  12.7 us
    slice x12, local copies, waits for them, and re-layouts, cross_rounded(): return jnp.concatenate([lowered[0:1], parts[1:2], lowered[2:3]], axis=0)  12.1 us
    broadcast_in_dim x7, local copies, waits for them, and re-layouts, forward_block(): raised = jnp.where(key_mask, jnp.exp(score_grid - row_max), 0.0)  11.6 us
  transfers between devices with their start and end apart: 10, of which 5 were waited for; matrix products, arithmetic and copies ran while one was open for 28% of the time, Pallas kernels for 0%

commit v1 on v0

v1 whole, which is shorter than its diff:
```python
import functools

import jax
import jax.numpy as jnp
from jax import lax
from jax.experimental import pallas as pl
from jax.experimental.pallas import tpu as pltpu
from jax.sharding import PartitionSpec as P

HEADS = 12
HD = 128
TILE = 384
TW = 2
SLOTS = 3 * TW
LAYER = TW * TILE
MESH = pl.DeviceIdType.MESH
LOG2E = 1.4426950408889634
VMEM_LIMIT = 56 * 1024 * 1024


def head_cols(at):
    return pl.ds(pl.multiple_of(at * HD, HD), HD)


def row_block(start, rows):
    return pl.ds(pl.multiple_of(start, rows), rows)


def greet(n_uly, n_ctx, uly_at, ctx_at):
    barrier = pltpu.get_barrier_semaphore()
    for step in range(1, n_uly):
        peer = lax.rem(uly_at + step, n_uly)
        pl.semaphore_signal(barrier, inc=1, device_id={"uly": peer}, device_id_type=MESH)

    @pl.when(ctx_at > 0)
    def _():
        pl.semaphore_signal(barrier, inc=1, device_id={"ctx": ctx_at - 1}, device_id_type=MESH)

    @pl.when(ctx_at < n_ctx - 1)
    def _():
        pl.semaphore_signal(barrier, inc=1, device_id={"ctx": ctx_at + 1}, device_id_type=MESH)

    interior = jnp.logical_and(ctx_at > 0, ctx_at < n_ctx - 1)
    pl.semaphore_wait(barrier, n_uly + interior.astype(jnp.int32))


def in_kernel(n_uly, n_ctx, heads, q, k, v, og, ow, qh, kw, vw, g,
              og_v, ow_v, load_sem, own_sem, send_sem, recv_sem, halo_send, halo_recv):
    uly_at, ctx_at = lax.axis_index("uly"), lax.axis_index("ctx")
    rows = q.shape[0]
    loads = [pltpu.make_async_copy(og, og_v, load_sem.at[0]),
             pltpu.make_async_copy(ow, ow_v, load_sem.at[1])]
    for load in loads:
        load.start()
    triples = ((k, kw, LAYER), (v, vw, LAYER), (q, qh, 0))
    own = {}
    for h in range(heads):
        for i, (src, dst, base) in enumerate(triples):
            own[h, i] = pltpu.make_async_copy(
                src.at[:, head_cols(uly_at * heads + h)],
                dst.at[h, row_block(base + uly_at * rows, rows)],
                own_sem.at[h, i])
            own[h, i].start()
    greet(n_uly, n_ctx, uly_at, ctx_at)

    def piece(h, i, step, owner):
        src, dst, base = triples[i]
        peer = lax.rem(uly_at + step, n_uly)
        return pltpu.make_async_remote_copy(
            src_ref=src.at[:, head_cols(peer * heads + h)],
            dst_ref=dst.at[h, row_block(base + owner * rows, rows)],
            send_sem=send_sem.at[h, i, step - 1],
            recv_sem=recv_sem.at[h, i, step - 1],
            device_id={"uly": peer}, device_id_type=MESH)

    order = [(h, i) for h in range(heads) for i in range(2)] + [(h, 2) for h in range(heads)]
    for h, i in order:
        for step in range(1, n_uly):
            piece(h, i, step, uly_at).start()

    for load in loads:
        load.wait()

    def grad_rows(at, carry):
        chunk = row_block(at * TILE, TILE)
        out = lax.dot_general(og_v[chunk, :], ow_v[...], (((1,), (1,)), ((), ())),
                              preferred_element_type=jnp.float32).astype(jnp.bfloat16)
        for h in range(heads):
            g[h, chunk, :] = out[:, h * HD:(h + 1) * HD]
        return carry

    lax.fori_loop(0, TW, grad_rows, 0)

    def arrived(h, i):
        own[h, i].wait()
        for step in range(1, n_uly):
            owner = lax.rem(uly_at + n_uly - step, n_uly)
            piece(h, i, step, owner).wait_recv()

    def halo(h, i, side):
        buf = triples[i][1]
        slot = 2 if side == 0 else 0
        return pltpu.make_async_remote_copy(
            src_ref=buf.at[h, pl.ds(LAYER, LAYER)],
            dst_ref=buf.at[h, pl.ds(slot * LAYER, LAYER)],
            send_sem=halo_send.at[h, i, side],
            recv_sem=halo_recv.at[h, i, side],
            device_id={"ctx": ctx_at - 1 if side == 0 else ctx_at + 1}, device_id_type=MESH)

    for h in range(heads):
        for i in range(2):
            arrived(h, i)

            @pl.when(ctx_at > 0)
            def _():
                halo(h, i, 0).start()

            @pl.when(ctx_at < n_ctx - 1)
            def _():
                halo(h, i, 1).start()

    for h in range(heads):
        arrived(h, 2)
    for h in range(heads):
        for i in range(2):
            @pl.when(ctx_at > 0)
            def _():
                halo(h, i, 0).wait_send()
                halo(h, i, 1).wait_recv()

            @pl.when(ctx_at < n_ctx - 1)
            def _():
                halo(h, i, 1).wait_send()
                halo(h, i, 0).wait_recv()
    for h, i in order:
        for step in range(1, n_uly):
            piece(h, i, step, uly_at).wait_send()


def gather_heads(q, k, v, og, ow, n_uly, n_ctx, heads):
    span = LAYER
    anywhere = pl.BlockSpec(memory_space=pl.ANY)
    return pl.pallas_call(
        functools.partial(in_kernel, n_uly, n_ctx, heads),
        out_shape=(jax.ShapeDtypeStruct((heads, span, HD), jnp.bfloat16),
                   jax.ShapeDtypeStruct((heads, 3 * span, HD), jnp.bfloat16),
                   jax.ShapeDtypeStruct((heads, 3 * span, HD), jnp.bfloat16),
                   jax.ShapeDtypeStruct((heads, span, HD), jnp.bfloat16)),
        in_specs=[anywhere] * 5,
        out_specs=(anywhere, anywhere, anywhere, pl.BlockSpec(memory_space=pltpu.VMEM)),
        scratch_shapes=[
            pltpu.VMEM(og.shape, jnp.bfloat16),
            pltpu.VMEM(ow.shape, jnp.bfloat16),
            pltpu.SemaphoreType.DMA((2,)),
            pltpu.SemaphoreType.DMA((heads, 3)),
            pltpu.SemaphoreType.DMA((heads, 3, n_uly - 1)),
            pltpu.SemaphoreType.DMA((heads, 3, n_uly - 1)),
            pltpu.SemaphoreType.DMA((heads, 2, 2)),
            pltpu.SemaphoreType.DMA((heads, 2, 2)),
        ],
        compiler_params=pltpu.CompilerParams(
            collective_id=0, has_side_effects=True, vmem_limit_bytes=VMEM_LIMIT),
        name="gather_heads",
    )(q, k, v, og, ow)


def lane_fold(x, op):
    out = x[:, 0:HD]
    for at in range(HD, x.shape[1], HD):
        out = op(out, x[:, at:at + HD])
    return out


def attend_kernel(allow, q, kw, vw, g, og, dq, own, edge, wpart,
                  s_buf, p_buf, m_buf, l_buf, o_buf, dq_buf, dk_buf, dv_buf, att):
    head = pl.program_id(0)
    scaling = HD ** (-0.5)
    dk_buf[...] = jnp.zeros_like(dk_buf)
    dv_buf[...] = jnp.zeros_like(dv_buf)
    nt = (((1,), (1,)), ((), ()))
    tn = (((0,), (0,)), ((), ()))

    def query_tile(spot, carry):
        rows = row_block(spot * TILE, TILE)
        flags = (head * TW + spot) * SLOTS

        def each(body):
            def step(slot, c):
                @pl.when(allow[flags + slot] > 0)
                def _():
                    body(slot, row_block(slot * TILE, TILE))
                return c
            lax.fori_loop(0, SLOTS, step, 0)

        m_buf[...] = jnp.full_like(m_buf, -jnp.inf)
        l_buf[...] = jnp.zeros_like(l_buf)
        o_buf[...] = jnp.zeros_like(o_buf)
        dq_buf[...] = jnp.zeros_like(dq_buf)

        def score(slot, keys):
            s = lax.dot_general(q[0, rows, :], kw[0, keys, :], nt, preferred_element_type=jnp.float32)
            s_buf[slot] = s
            m_buf[...] = jnp.maximum(m_buf[...], lane_fold(s, jnp.maximum))

        each(score)
        top = jnp.max(m_buf[...], axis=1, keepdims=True)

        def weigh(slot, keys):
            p = jnp.exp2((s_buf[slot] - top) * (scaling * LOG2E))
            l_buf[...] += lane_fold(p, jnp.add)
            low = p.astype(jnp.bfloat16)
            p_buf[slot] = low
            o_buf[...] += jnp.dot(low, vw[0, keys, :], preferred_element_type=jnp.float32)

        each(weigh)
        inv = 1.0 / jnp.sum(l_buf[...], axis=1, keepdims=True)
        out = o_buf[...] * inv
        att[rows, :] = out.astype(jnp.bfloat16)
        gp = (g[0, rows, :].astype(jnp.float32) * inv).astype(jnp.bfloat16)
        delta = jnp.sum(out * gp.astype(jnp.float32), axis=1, keepdims=True)

        def back(slot, keys):
            low = p_buf[slot]
            dp = lax.dot_general(gp, vw[0, keys, :], nt, preferred_element_type=jnp.float32)
            ds = (low.astype(jnp.float32) * (dp - delta)).astype(jnp.bfloat16)
            dv_buf[keys, :] += lax.dot_general(low, gp, tn, preferred_element_type=jnp.float32)
            dk_buf[keys, :] += lax.dot_general(ds, q[0, rows, :], tn, preferred_element_type=jnp.float32)
            dq_buf[...] += jnp.dot(ds, kw[0, keys, :], preferred_element_type=jnp.float32)

        each(back)
        dq[0, rows, :] = (dq_buf[...] * scaling).astype(jnp.bfloat16)
        return carry

    lax.fori_loop(0, TW, query_tile, 0)
    own[0, 0] = dk_buf[LAYER:2 * LAYER, :] * scaling
    own[0, 1] = dv_buf[LAYER:2 * LAYER, :]
    for side in range(2):
        part = slice(2 * side * LAYER, (2 * side + 1) * LAYER)
        edge[0, side, 0] = (dk_buf[part, :] * scaling).astype(jnp.bfloat16)
        edge[0, side, 1] = dv_buf[part, :].astype(jnp.bfloat16)
    width = 2 * TILE

    def weight_cols(at, carry):
        cols = row_block(at * width, width)
        wpart[:, cols] = lax.dot_general(
            att[...], og[:, cols], tn, preferred_element_type=jnp.float32).astype(wpart.dtype)
        return carry

    lax.fori_loop(0, og.shape[1] // width, weight_cols, 0)


def attend(allow, q, kw, vw, g, og, heads):
    def per_head(*dims):
        return pl.BlockSpec((1,) + dims, lambda h, allow: (h,) + (0,) * len(dims))

    dout = og.shape[1]
    grid_spec = pltpu.PrefetchScalarGridSpec(
        num_scalar_prefetch=1,
        grid=(heads,),
        in_specs=[per_head(LAYER, HD), per_head(3 * LAYER, HD), per_head(3 * LAYER, HD),
                  per_head(LAYER, HD), pl.BlockSpec((LAYER, dout), lambda h, allow: (0, 0))],
        out_specs=[per_head(LAYER, HD), per_head(2, LAYER, HD), per_head(2, 2, LAYER, HD),
                   pl.BlockSpec((HD, dout), lambda h, allow: (h, 0))],
        scratch_shapes=[
            pltpu.VMEM((SLOTS, TILE, TILE), jnp.float32),
            pltpu.VMEM((SLOTS, TILE, TILE), jnp.bfloat16),
            pltpu.VMEM((TILE, HD), jnp.float32),
            pltpu.VMEM((TILE, HD), jnp.float32),
            pltpu.VMEM((TILE, HD), jnp.float32),
            pltpu.VMEM((TILE, HD), jnp.float32),
            pltpu.VMEM((3 * LAYER, HD), jnp.float32),
            pltpu.VMEM((3 * LAYER, HD), jnp.float32),
            pltpu.VMEM((LAYER, HD), jnp.bfloat16),
        ])
    return pl.pallas_call(
        attend_kernel,
        out_shape=(jax.ShapeDtypeStruct((heads, LAYER, HD), jnp.bfloat16),
                   jax.ShapeDtypeStruct((heads, 2, LAYER, HD), jnp.float32),
                   jax.ShapeDtypeStruct((heads, 2, 2, LAYER, HD), jnp.bfloat16),
                   jax.ShapeDtypeStruct((heads * HD, dout), jnp.bfloat16)),
        grid_spec=grid_spec,
        compiler_params=pltpu.CompilerParams(vmem_limit_bytes=VMEM_LIMIT),
        name="attend",
    )(allow, q, kw, vw, g, og)


def out_kernel(n_uly, n_ctx, heads, dqh, own, edge, dq, dk, dv,
               inbox, low, own_sem, send_sem, recv_sem, halo_send, halo_recv):
    uly_at, ctx_at = lax.axis_index("uly"), lax.axis_index("ctx")
    rows = dq.shape[0]
    greet(n_uly, n_ctx, uly_at, ctx_at)

    def source(h, i):
        return dqh.at[h] if i == 2 else low.at[h, i]

    targets = (dk, dv, dq)

    def piece(h, i, step, owner):
        peer = lax.rem(uly_at + step, n_uly)
        return pltpu.make_async_remote_copy(
            src_ref=source(h, i).at[row_block(peer * rows, rows)],
            dst_ref=targets[i].at[:, head_cols(owner * heads + h)],
            send_sem=send_sem.at[h, i, step - 1],
            recv_sem=recv_sem.at[h, i, step - 1],
            device_id={"uly": peer}, device_id_type=MESH)

    def own_piece(h, i):
        return pltpu.make_async_copy(
            source(h, i).at[row_block(uly_at * rows, rows)],
            targets[i].at[:, head_cols(uly_at * heads + h)], own_sem.at[h, i])

    def halo(h, side):
        return pltpu.make_async_remote_copy(
            src_ref=edge.at[h, side],
            dst_ref=inbox.at[h, 1 - side],
            send_sem=halo_send.at[h, side],
            recv_sem=halo_recv.at[h, side],
            device_id={"ctx": ctx_at - 1 if side == 0 else ctx_at + 1}, device_id_type=MESH)

    def send_out(h, i):
        for step in range(1, n_uly):
            piece(h, i, step, uly_at).start()
        own_piece(h, i).start()

    for h in range(heads):
        @pl.when(ctx_at > 0)
        def _():
            halo(h, 0).start()

        @pl.when(ctx_at < n_ctx - 1)
        def _():
            halo(h, 1).start()

    for h in range(heads):
        send_out(h, 2)
    for h in range(heads):
        @pl.when(ctx_at == 0)
        def _():
            halo(h, 0).wait_recv()
            low[h] = (own[h] + inbox[h, 1].astype(jnp.float32)).astype(jnp.bfloat16)

        @pl.when(ctx_at == n_ctx - 1)
        def _():
            halo(h, 1).wait_recv()
            low[h] = (own[h] + inbox[h, 0].astype(jnp.float32)).astype(jnp.bfloat16)

        @pl.when(jnp.logical_and(ctx_at > 0, ctx_at < n_ctx - 1))
        def _():
            halo(h, 0).wait_recv()
            halo(h, 1).wait_recv()
            both = inbox[h, 0].astype(jnp.float32) + inbox[h, 1].astype(jnp.float32)
            low[h] = (own[h] + both).astype(jnp.bfloat16)

        for i in range(2):
            send_out(h, i)
    for h in range(heads):
        for i in range(3):
            for step in range(1, n_uly):
                owner = lax.rem(uly_at + n_uly - step, n_uly)
                piece(h, i, step, owner).wait_recv()
                piece(h, i, step, uly_at).wait_send()
            own_piece(h, i).wait()

        @pl.when(ctx_at > 0)
        def _():
            halo(h, 0).wait_send()

        @pl.when(ctx_at < n_ctx - 1)
        def _():
            halo(h, 1).wait_send()


def scatter_tokens(dqh, own, edge, rows, n_uly, n_ctx, heads):
    anywhere = pl.BlockSpec(memory_space=pl.ANY)
    shape = jax.ShapeDtypeStruct((rows, n_uly * heads * HD), jnp.bfloat16)
    return pl.pallas_call(
        functools.partial(out_kernel, n_uly, n_ctx, heads),
        out_shape=(shape,) * 3,
        in_specs=[anywhere, pl.BlockSpec(memory_space=pltpu.VMEM), anywhere],
        out_specs=(anywhere,) * 3,
        scratch_shapes=[
            pltpu.VMEM((heads, 2, 2, LAYER, HD), jnp.bfloat16),
            pltpu.VMEM((heads, 2, LAYER, HD), jnp.bfloat16),
            pltpu.SemaphoreType.DMA((heads, 3)),
            pltpu.SemaphoreType.DMA((heads, 3, n_uly - 1)),
            pltpu.SemaphoreType.DMA((heads, 3, n_uly - 1)),
            pltpu.SemaphoreType.DMA((heads, 2)),
            pltpu.SemaphoreType.DMA((heads, 2)),
        ],
        compiler_params=pltpu.CompilerParams(
            collective_id=1, has_side_effects=True, vmem_limit_bytes=VMEM_LIMIT),
        cost_estimate=pl.CostEstimate(flops=10 ** 10, bytes_accessed=10 ** 8, transcendentals=0),
        name="scatter_tokens",
    )(dqh, own, edge)


def allowed_tiles(tile_lists, windows, heads):
    ctx_at, uly_at = lax.axis_index("ctx"), lax.axis_index("uly")
    listed = lax.dynamic_slice_in_dim(tile_lists, ctx_at * TW, TW, 0) >= 0
    reach = lax.dynamic_slice_in_dim(windows, uly_at * heads, heads, 0)
    slot_ids = jnp.arange(SLOTS, dtype=jnp.int32)
    spot_ids = jnp.arange(TW, dtype=jnp.int32)
    near_time = jnp.abs(slot_ids // TW - 1)[None, :] <= reach[:, 0:1]
    far = jnp.abs(slot_ids[None, :] % TW - spot_ids[:, None])
    near_space = far[None] <= reach[:, 1][:, None, None]
    allowed = listed[None] & near_time[:, None, :] & near_space
    return allowed.astype(jnp.int32).reshape(-1)


def on_device(queries, key_rows, value_rows, out_grad, out_weight, tile_lists, windows):
    n_uly, n_ctx = lax.axis_size("uly"), lax.axis_size("ctx")
    heads = HEADS // n_uly
    rows = queries.shape[1]
    qh, kw, vw, g = gather_heads(
        queries[0], key_rows[0], value_rows[0], out_grad[0], out_weight, n_uly, n_ctx, heads)
    allow = allowed_tiles(tile_lists, windows, heads)
    dqh, own, edge, wpart = attend(allow, qh, kw, vw, g, out_grad[0], heads)
    total = lax.psum(wpart, ("dp", "ctx"))
    weight_grad = (total.astype(jnp.float32) / lax.axis_size("dp")).astype(jnp.bfloat16)
    dq, dk, dv = scatter_tokens(dqh, own, edge, rows, n_uly, n_ctx, heads)
    return (dq[None], dk[None], dv[None], weight_grad)


def solution(mesh):
    tokens = P("dp", ("ctx", "uly"), None)
    in_specs = (tokens, tokens, tokens, P("dp", "ctx", None), P("uly", None), P(), P())
    out_specs = (tokens, tokens, tokens, P("uly", None))
    return jax.shard_map(
        on_device, mesh=mesh, in_specs=in_specs, out_specs=out_specs, check_vma=False
    )
```

time: 337 us -> 169 us (0.50); the launches traced: 332 us -> 171 us
  Pallas kernels: 0 us -> 126 us
  local copies, waits for them, and re-layouts: 94.7 us -> 3.74 us
  matrix products: 60.8 us -> 0 us
  waiting for transfers between devices: 81.8 us -> 22.5 us
  other arithmetic: 44.8 us -> 4.43 us
  starting transfers between devices: 34.3 us -> 0.04 us
    pallas_call x0 -> x3, Pallas kernels: none -> 126 us  [the longest x1 50.4 us: scatter_tokens(): pl.pallas_call(functools.partial(out_kernel, n_uly, n_ctx, heads), out_sh...]
    dot_general x20 -> x0, matrix products: 60.8 us -> none  [the longest x3 14.9 us: backward_block(): jnp.dot(grad_tile, value_window.T, preferred_element_type=jnp.float32)]
    all_to_all x5 -> x0, waiting for transfers between devices: 44.2 us -> none  [the longest x1 21.1 us: on_device(): lax.all_to_all(jnp.stack([key_rows, value_rows]), 'uly', split_axis=3, co...]
    all_to_all x5 -> x0, starting transfers between devices: 24.1 us -> none  [the longest x1 6.45 us: on_device(): lax.all_to_all(jnp.stack([key_rows, value_rows]), 'uly', split_axis=3, co...]
    slice x21 -> x0, local copies, waits for them, and re-layouts: 23.9 us -> none  [the longest x12 12.1 us: cross_rounded(): return jnp.concatenate([lowered[0:1], parts[1:2], lowered[2:3]], axis=0)]
    unnamed x4 -> x0, other arithmetic: 22.5 us -> none
    unnamed x109 -> x11, local copies, waits for them, and re-layouts: 19.3 us -> 3.07 us
    psum x1, waiting for transfers between devices: 37.6 us -> 22.4 us  [on_device(): total = lax.psum(wpart, ('dp', 'ctx'))]
  transfers between devices with their start and end apart: 10 -> 1, of which waited for: 5 -> 1; matrix products, arithmetic and copies ran while one was open for 28% -> 0% of each run, Pallas kernels for 0% -> 29%
where the time goes in v1:
time: 169 us; the launch traced here: 171 us
  Pallas kernels  126 us (75%)
  waiting for transfers between devices  22.5 us (13%)
  between operations  14.1 us (8%)
  other arithmetic  4.43 us (3%)
  local copies, waits for them, and re-layouts  3.74 us (2%)
    pallas_call x1, Pallas kernels, scatter_tokens(): pl.pallas_call(functools.partial(out_kernel, n_uly, n_ctx, heads), out_sh...  50.4 us
    pallas_call x1, Pallas kernels, gather_heads(): pl.pallas_call(functools.partial(in_kernel, n_uly, n_ctx, heads), out_sha...  46 us
    pallas_call x1, Pallas kernels, attend(): pl.pallas_call(attend_kernel, out_shape=(jax.ShapeDtypeStruct((heads, LAY...  29.8 us
    psum x1, waiting for transfers between devices, on_device(): total = lax.psum(wpart, ('dp', 'ctx'))  22.4 us
    convert_element_type x1, other arithmetic, on_device(): (total.astype(jnp.float32) / lax.axis_size('dp')).astype(jnp.bfloat16)  3.57 us
  transfers between devices with their start and end apart: 1, of which 1 were waited for; matrix products, arithmetic and copies ran while one was open for 0% of the time, Pallas kernels for 29%

profile of v1, /device:TPU:0, one launch (start us, length us, event | category | flops | bytes accessed | tf_op | source)
XLA Modules:
  0.0 170.8 jit_solution(10031596715488359279)
XLA Ops:
  7.2 0.0 copy-start
  7.2 0.0 all-reduce.2.cloned.1.call-start
  7.2 0.6 copy-done
  7.8 0.1 constant_dynamic-slice_fusion
  7.9 0.7 dynamic-slice_compare_fusion
  8.6 0.1 broadcast_compare_fusion
  8.7 0.1 and_convert_fusion
  8.8 0.6 reshape.95.allow
  9.4 46.0 %gather_heads.1 = (bf16[3,768,128]{2,1,0:T(8,128)(2,1)}, bf16[3,2304,128]{2,1,0:T(8,128)(2,1)}, bf16[3,2304,128]{2,1,0:T(8,128)(2,1)}, bf16[3,768,128]{2,1,0:T(8,128)(2,1)}) custom-call(bf16[192,1536]{1,0:T(8,128)(2,1)} %bitcast.13, bf16[192,1536]{1,0:T(8,128)(2,1)} %bitcast.14, bf16[192,1536]{1,0:T(8,128)(2,1)} %bitcast.15, bf16[768,3072]{1,0:T(8,128)(2,1)} %bitcast.11, ...), custom_call_target="tpu_custom_call" | custom-call | tf_op jit(solution)/shard_map/gather_heads/pallas_call | solution.py:143
  55.3 29.8 %attend.1 = (bf16[3,768,128]{2,1,0:T(8,128)(2,1)}, f32[3,2,768,128]{3,2,1,0:T(8,128)}, bf16[3,2,2,768,128]{4,3,2,1,0:T(8,128)(2,1)}, bf16[384,3072]{1,0:T(8,128)(2,1)}) custom-call(s32[36]{0:T(128)} %reshape.95.allow, bf16[3,768,128]{2,1,0:T(8,128)(2,1)} %get-tuple-element.15.q, bf16[3,2304,128]{2,1,0:T(8,128)(2,1)} %get-tuple-element.16.kw, ...), custom_call_target="tpu_custom_call" | custom-call | tf_op jit(solution)/shard_map/attend/pallas_call | solution.py:275
  85.1 0.0 all-reduce.2.cloned.1.call-update
  85.1 50.4 %scatter_tokens.1 = (bf16[192,1536]{1,0:T(8,128)(2,1)}, bf16[192,1536]{1,0:T(8,128)(2,1)}, bf16[192,1536]{1,0:T(8,128)(2,1)}) custom-call(bf16[3,768,128]{2,1,0:T(8,128)(2,1)} %get-tuple-element.19.dqh, f32[3,2,768,128]{3,2,1,0:T(8,128)} %get-tuple-element.20.own, bf16[3,2,2,768,128]{4,3,2,1,0:T(8,128)(2,1)} %get-tuple-element.21.edge), custom_call_target="tpu_custom_call" | custom-call | flops 10000000000 | bytes 100000000 | tf_op jit(solution)/shard_map/scatter_tokens/pallas_call | solution.py:376
  135.5 0.0 copy-start.3
  135.5 0.0 copy-start.2
  135.5 22.4 %all-reduce.2.cloned.1.call-done = bf16[384,3072]{1,0:T(8,128)(2,1)} async-done(((bf16[384,3072]{1,0:T(8,128)(2,1)}), bf16[384,3072]{1,0:T(8,128)(2,1)}) %all-reduce.2.cloned.1.call-update) | async-done | bytes 2359312 | tf_op jit(solution)/shard_map/psum | solution.py:418
  158.0 3.6 %multiply_convert_fusion = bf16[384,3072]{1,0:T(8,128)(2,1)} fusion(bf16[384,3072]{1,0:T(8,128)(2,1)} %all-reduce.2.cloned.1.call-done), kind=kLoop, calls=%fused_computation | loop fusion | flops 3538944 | bytes 4718592 | tf_op jit(solution)/shard_map/convert_element_type | solution.py:419
  161.5 0.0 copy-done.3
  161.5 0.0 copy-start.1
  161.5 0.8 copy.15
  162.4 0.0 copy-done.2
  162.4 0.8 copy.16
  163.2 0.0 copy-done.1
  163.2 0.8 copy.17
  (3 shorter events, 0.0 us)
Async XLA Ops:
  7.2 0.7 copy-start
  7.2 150.8 %all-reduce.2.cloned.1.call-start = ((), (), s32[]{:S(2)}) async-start(), calls=%async_computation | async-start | bytes 4718592 | tf_op jit(solution)/shard_map/psum | solution.py:418
  135.5 26.0 %copy-start.3 = (bf16[192,1536]{1,0:T(8,128)(2,1)S(1)}, bf16[192,1536]{1,0:T(8,128)(2,1)}, u32[]{:S(2)}) copy-start(bf16[192,1536]{1,0:T(8,128)(2,1)} %get-tuple-element.22) | copy-start | bytes 1769476
  135.5 26.8 %copy-start.2 = (bf16[192,1536]{1,0:T(8,128)(2,1)S(1)}, bf16[192,1536]{1,0:T(8,128)(2,1)}, u32[]{:S(2)}) copy-start(bf16[192,1536]{1,0:T(8,128)(2,1)} %get-tuple-element.23) | copy-start | bytes 1769476
  161.5 1.6 copy-start.1
Sparse Core Ops, SparseCore 0:
  85.3 72.6 all-reduce.1

commit v2 on v1

--- a/solution.py
+++ b/solution.py
@@ -42,6 +42,16 @@
 
     interior = jnp.logical_and(ctx_at > 0, ctx_at < n_ctx - 1)
     pl.semaphore_wait(barrier, n_uly + interior.astype(jnp.int32))
+
+
+def greet_groups(sizes):
+    barrier = pltpu.get_barrier_semaphore()
+    for axis, count in sizes:
+        at = lax.axis_index(axis)
+        for step in range(1, count):
+            pl.semaphore_signal(barrier, inc=1, device_id={axis: lax.rem(at + step, count)},
+                                device_id_type=MESH)
+    pl.semaphore_wait(barrier, sum(count - 1 for _, count in sizes))
 
 
 def in_kernel(n_uly, n_ctx, heads, q, k, v, og, ow, qh, kw, vw, g,
@@ -284,11 +294,133 @@
     )(allow, q, kw, vw, g, og)
 
 
-def out_kernel(n_uly, n_ctx, heads, dqh, own, edge, dq, dk, dv,
-               inbox, low, own_sem, send_sem, recv_sem, halo_send, halo_recv):
+def chunk_of(n_dp, dout):
+    bands = 1 if (dout // n_dp) % 128 == 0 else 2
+    return bands, HD // 4 // bands, dout * bands // n_dp
+
+
+class WeightSum:
+    def __init__(self, n_dp, part, out, in1, sum1, in2, sum2, in3, final, sems, dp_sems, own_sem):
+        self.n_dp, self.part, self.out = n_dp, part, out
+        self.in1, self.sum1, self.in2, self.sum2, self.in3, self.final = in1, sum1, in2, sum2, in3, final
+        self.sems, self.dp_sems, self.own_sem = sems, dp_sems, own_sem
+        ctx_at = lax.axis_index("ctx")
+        self.dp_at = lax.axis_index("dp")
+        self.core, self.far = lax.rem(ctx_at, 2), ctx_at // 2
+        self.core_peer = ctx_at + 1 - 2 * self.core
+        self.far_peer = lax.rem(ctx_at + 2, 4)
+        self.bands, self.height, self.width = chunk_of(n_dp, part.shape[1])
+
+    def cols(self, at):
+        return pl.ds(pl.multiple_of((at // self.bands) * self.width, self.width), self.width)
+
+    def band(self, at):
+        return row_block(lax.rem(at, self.bands) * self.height, self.height)
+
+    def chunk_rows(self, h, at):
+        start = h * HD + self.core * (HD // 2) + self.far * (HD // 4)
+        return row_block(start + lax.rem(at, self.bands) * self.height, self.height)
+
+    def copy(self, kind, h, src, dst, peer):
+        return pltpu.make_async_remote_copy(
+            src_ref=src, dst_ref=dst, send_sem=self.sems.at[0, kind, h],
+            recv_sem=self.sems.at[1, kind, h], device_id={"ctx": peer}, device_id_type=MESH)
+
+    def dp_copy(self, kind, h, step, src, dst):
+        return pltpu.make_async_remote_copy(
+            src_ref=src, dst_ref=dst, send_sem=self.dp_sems.at[0, kind, h, step - 1],
+            recv_sem=self.dp_sems.at[1, kind, h, step - 1],
+            device_id={"dp": lax.rem(self.dp_at + step, self.n_dp)}, device_id_type=MESH)
+
+    def core_rows(self, h, core):
+        return row_block(h * HD + core * (HD // 2), HD // 2)
+
+    def far_rows(self, h, far):
+        return row_block(h * HD + self.core * (HD // 2) + far * (HD // 4), HD // 4)
+
+    def reduce1(self, h):
+        return self.copy(0, h, self.part.at[self.core_rows(h, 1 - self.core)], self.in1.at[h],
+                         self.core_peer)
+
+    def reduce2(self, h):
+        return self.copy(1, h, self.sum1.at[h, row_block((1 - self.far) * (HD // 4), HD // 4)],
+                         self.in2.at[h], self.far_peer)
+
+    def reduce3(self, h, step):
+        peer = lax.rem(self.dp_at + step, self.n_dp)
+        return self.dp_copy(0, h, step, self.sum2.at[h, self.band(peer), self.cols(peer)],
+                            self.in3.at[h, step - 1])
+
+    def share1(self, h, step, owner):
+        return self.dp_copy(1, h, step, self.final.at[h],
+                            self.out.at[self.chunk_rows(h, owner), self.cols(owner)])
+
+    def own_copy(self, h):
+        return pltpu.make_async_copy(
+            self.final.at[h], self.out.at[self.chunk_rows(h, self.dp_at), self.cols(self.dp_at)],
+            self.own_sem.at[h])
+
+    def share2(self, h, far):
+        rows = self.far_rows(h, far)
+        return self.copy(2, h, self.out.at[rows], self.out.at[rows], self.far_peer)
+
+    def share3(self, h, core):
+        rows = self.core_rows(h, core)
+        return self.copy(3, h, self.out.at[rows], self.out.at[rows], self.core_peer)
+
+    def step0(self, h):
+        self.reduce1(h).start()
+
+    def step1(self, h):
+        self.reduce1(h).wait_recv()
+        mine = self.part[self.core_rows(h, self.core), :].astype(jnp.float32)
+        self.sum1[h] = (mine + self.in1[h].astype(jnp.float32)).astype(jnp.bfloat16)
+        self.reduce2(h).start()
+
+    def step2(self, h):
+        self.reduce2(h).wait_recv()
+        mine = self.sum1[h, row_block(self.far * (HD // 4), HD // 4), :].astype(jnp.float32)
+        self.sum2[h] = (mine + self.in2[h].astype(jnp.float32)).astype(jnp.bfloat16)
+        for step in range(1, self.n_dp):
+            self.reduce3(h, step).start()
+
+    def step3(self, h):
+        total = self.sum2[h, self.band(self.dp_at), self.cols(self.dp_at)].astype(jnp.float32)
+        for step in range(1, self.n_dp):
+            self.reduce3(h, step).wait_recv()
+            total = total + self.in3[h, step - 1].astype(jnp.float32)
+        self.final[h] = (total / self.n_dp).astype(jnp.bfloat16)
+        self.own_copy(h).start()
+        for step in range(1, self.n_dp):
+            self.share1(h, step, self.dp_at).start()
+
+    def step4(self, h):
+        self.own_copy(h).wait()
+        for step in range(1, self.n_dp):
+            self.share1(h, step, lax.rem(self.dp_at + self.n_dp - step, self.n_dp)).wait_recv()
+        self.share2(h, self.far).start()
+
+    def step5(self, h):
+        self.share2(h, 1 - self.far).wait_recv()
+        self.share3(h, self.core).start()
+
+    def finish(self, h):
+        self.share3(h, 1 - self.core).wait_recv()
+        self.share3(h, self.core).wait_send()
+        self.share2(h, self.far).wait_send()
+        self.reduce1(h).wait_send()
+        self.reduce2(h).wait_send()
+        for step in range(1, self.n_dp):
+            self.reduce3(h, step).wait_send()
+            self.share1(h, step, self.dp_at).wait_send()
+
+
+def out_kernel(n_dp, n_uly, n_ctx, heads, dqh, own, edge, wpart, dq, dk, dv, wout,
+               inbox, low, own_sem, send_sem, recv_sem, halo_send, halo_recv, *weight_refs):
     uly_at, ctx_at = lax.axis_index("uly"), lax.axis_index("ctx")
     rows = dq.shape[0]
-    greet(n_uly, n_ctx, uly_at, ctx_at)
+    weight = WeightSum(n_dp, wpart, wout, *weight_refs)
+    greet_groups((("uly", n_uly), ("ctx", n_ctx), ("dp", n_dp)))
 
     def source(h, i):
         return dqh.at[h] if i == 2 else low.at[h, i]
@@ -332,7 +464,11 @@
             halo(h, 1).start()
 
     for h in range(heads):
+        weight.step0(h)
+    for h in range(heads):
         send_out(h, 2)
+    for h in range(heads):
+        weight.step1(h)
     for h in range(heads):
         @pl.when(ctx_at == 0)
         def _():
@@ -353,6 +489,13 @@
 
         for i in range(2):
             send_out(h, i)
+    stages = (weight.step2, weight.step3, weight.step4, weight.step5)
+    for at in range(heads + len(stages) - 1):
+        for lag, stage in enumerate(stages):
+            if 0 <= at - lag < heads:
+                stage(at - lag)
+    for h in range(heads):
+        weight.finish(h)
     for h in range(heads):
         for i in range(3):
             for step in range(1, n_uly):
@@ -370,14 +513,17 @@
             halo(h, 1).wait_send()
 
 
-def scatter_tokens(dqh, own, edge, rows, n_uly, n_ctx, heads):
+def scatter_tokens(dqh, own, edge, wpart, rows, n_dp, n_uly, n_ctx, heads):
     anywhere = pl.BlockSpec(memory_space=pl.ANY)
+    dout = wpart.shape[1]
+    _, height, width = chunk_of(n_dp, dout)
     shape = jax.ShapeDtypeStruct((rows, n_uly * heads * HD), jnp.bfloat16)
     return pl.pallas_call(
-        functools.partial(out_kernel, n_uly, n_ctx, heads),
-        out_shape=(shape,) * 3,
-        in_specs=[anywhere, pl.BlockSpec(memory_space=pltpu.VMEM), anywhere],
-        out_specs=(anywhere,) * 3,
+        functools.partial(out_kernel, n_dp, n_uly, n_ctx, heads),
+        out_shape=(shape,) * 3 + (jax.ShapeDtypeStruct(wpart.shape, jnp.bfloat16),),
+        in_specs=[anywhere, pl.BlockSpec(memory_space=pltpu.VMEM), anywhere,
+                  pl.BlockSpec(memory_space=pltpu.VMEM)],
+        out_specs=(anywhere,) * 4,
         scratch_shapes=[
             pltpu.VMEM((heads, 2, 2, LAYER, HD), jnp.bfloat16),
             pltpu.VMEM((heads, 2, LAYER, HD), jnp.bfloat16),
@@ -386,12 +532,20 @@
             pltpu.SemaphoreType.DMA((heads, 3, n_uly - 1)),
             pltpu.SemaphoreType.DMA((heads, 2)),
             pltpu.SemaphoreType.DMA((heads, 2)),
+            pltpu.VMEM((heads, HD // 2, dout), jnp.bfloat16),
+            pltpu.VMEM((heads, HD // 2, dout), jnp.bfloat16),
+            pltpu.VMEM((heads, HD // 4, dout), jnp.bfloat16),
+            pltpu.VMEM((heads, HD // 4, dout), jnp.bfloat16),
+            pltpu.VMEM((heads, n_dp - 1, height, width), jnp.bfloat16),
+            pltpu.VMEM((heads, height, width), jnp.bfloat16),
+            pltpu.SemaphoreType.DMA((2, 4, heads)),
+            pltpu.SemaphoreType.DMA((2, 2, heads, n_dp - 1)),
+            pltpu.SemaphoreType.DMA((heads,)),
         ],
         compiler_params=pltpu.CompilerParams(
             collective_id=1, has_side_effects=True, vmem_limit_bytes=VMEM_LIMIT),
-        cost_estimate=pl.CostEstimate(flops=10 ** 10, bytes_accessed=10 ** 8, transcendentals=0),
         name="scatter_tokens",
-    )(dqh, own, edge)
+    )(dqh, own, edge, wpart)
 
 
 def allowed_tiles(tile_lists, windows, heads):
@@ -415,9 +569,8 @@
         queries[0], key_rows[0], value_rows[0], out_grad[0], out_weight, n_uly, n_ctx, heads)
     allow = allowed_tiles(tile_lists, windows, heads)
     dqh, own, edge, wpart = attend(allow, qh, kw, vw, g, out_grad[0], heads)
-    total = lax.psum(wpart, ("dp", "ctx"))
-    weight_grad = (total.astype(jnp.float32) / lax.axis_size("dp")).astype(jnp.bfloat16)
-    dq, dk, dv = scatter_tokens(dqh, own, edge, rows, n_uly, n_ctx, heads)
+    dq, dk, dv, weight_grad = scatter_tokens(
+        dqh, own, edge, wpart, rows, lax.axis_size("dp"), n_uly, n_ctx, heads)
     return (dq[None], dk[None], dv[None], weight_grad)
 
 

time: 169 us -> 151 us (0.89); the launches traced: 171 us -> 150 us
  waiting for transfers between devices: 22.5 us -> 0 us
  Pallas kernels: 126 us -> 140 us
  between operations: 14.1 us -> 0.68 us
  local copies, waits for them, and re-layouts: 3.74 us -> 7.99 us
  other arithmetic: 4.43 us -> 0.86 us
    psum x1 -> x0, waiting for transfers between devices: 22.4 us -> none  [on_device(): total = lax.psum(wpart, ('dp', 'ctx'))]
    pallas_call x1, Pallas kernels: 50.4 us -> 64.5 us  [scatter_tokens(): pl.pallas_call(functools.partial(out_kernel, n_dp, n_uly, n_ctx, heads),...]
    unnamed x11 -> x8, local copies, waits for them, and re-layouts: 3.07 us -> 7.32 us
    convert_element_type x1 -> x0, other arithmetic: 3.57 us -> none  [on_device(): (total.astype(jnp.float32) / lax.axis_size('dp')).astype(jnp.bfloat16)]
  transfers between devices with their start and end apart: 1 -> 0, of which waited for: 1 -> 0; matrix products, arithmetic and copies ran while one was open for 0% -> 0% of each run, Pallas kernels for 29% -> 0%
where the time goes in v2:
time: 151 us; the launch traced here: 150 us
  Pallas kernels  140 us (93%)
  local copies, waits for them, and re-layouts  7.99 us (5%)
    pallas_call x1, Pallas kernels, scatter_tokens(): pl.pallas_call(functools.partial(out_kernel, n_dp, n_uly, n_ctx, heads),...  64.5 us
    pallas_call x1, Pallas kernels, gather_heads(): pl.pallas_call(functools.partial(in_kernel, n_uly, n_ctx, heads), out_sha...  46 us
    pallas_call x1, Pallas kernels, attend(): pl.pallas_call(attend_kernel, out_shape=(jax.ShapeDtypeStruct((heads, LAY...  29.6 us
    unnamed x8, local copies, waits for them, and re-layouts  7.32 us

profile of v2, /device:TPU:0, one launch (start us, length us, event | category | flops | bytes accessed | tf_op | source)
XLA Modules:
  0.0 149.6 jit_solution(2471942411000123898)
XLA Ops:
  0.6 0.0 copy-start
  0.7 0.7 dynamic-slice_compare_fusion
  1.4 0.0 copy-done
  1.4 0.1 constant_dynamic-slice_fusion
  1.4 0.1 broadcast_compare_fusion
  1.5 0.1 and_convert_fusion
  1.6 0.6 reshape.95.allow
  2.2 46.0 %gather_heads.1 = (bf16[3,768,128]{2,1,0:T(8,128)(2,1)}, bf16[3,2304,128]{2,1,0:T(8,128)(2,1)}, bf16[3,2304,128]{2,1,0:T(8,128)(2,1)}, bf16[3,768,128]{2,1,0:T(8,128)(2,1)}) custom-call(bf16[192,1536]{1,0:T(8,128)(2,1)} %bitcast.13, bf16[192,1536]{1,0:T(8,128)(2,1)} %bitcast.14, bf16[192,1536]{1,0:T(8,128)(2,1)} %bitcast.15, bf16[768,3072]{1,0:T(8,128)(2,1)} %bitcast.11, ...), custom_call_target="tpu_custom_call" | custom-call | tf_op jit(solution)/shard_map/gather_heads/pallas_call | solution.py:153
  48.2 29.6 %attend.1 = (bf16[3,768,128]{2,1,0:T(8,128)(2,1)}, f32[3,2,768,128]{3,2,1,0:T(8,128)}, bf16[3,2,2,768,128]{4,3,2,1,0:T(8,128)(2,1)}, bf16[384,3072]{1,0:T(8,128)(2,1)}) custom-call(s32[36]{0:T(128)} %reshape.95.allow, bf16[3,768,128]{2,1,0:T(8,128)(2,1)} %get-tuple-element.16.q, bf16[3,2304,128]{2,1,0:T(8,128)(2,1)} %get-tuple-element.17.kw, ...), custom_call_target="tpu_custom_call" | custom-call | tf_op jit(solution)/shard_map/attend/pallas_call | solution.py:285
  77.8 64.5 %scatter_tokens.1 = (bf16[192,1536]{1,0:T(8,128)(2,1)}, bf16[192,1536]{1,0:T(8,128)(2,1)}, bf16[192,1536]{1,0:T(8,128)(2,1)}, bf16[384,3072]{1,0:T(8,128)(2,1)}) custom-call(bf16[3,768,128]{2,1,0:T(8,128)(2,1)} %get-tuple-element.20.dqh, f32[3,2,768,128]{3,2,1,0:T(8,128)} %get-tuple-element.21.own, bf16[3,2,2,768,128]{4,3,2,1,0:T(8,128)(2,1)} %get-tuple-element.22.edge, ...), custom_call_target="tpu_custom_call" | custom-call | tf_op jit(solution)/shard_map/scatter_tokens/pallas_call | solution.py:521
  142.3 0.0 copy-start.1
  142.3 2.1 %copy.15 = bf16[1,192,1536]{2,1,0:T(8,128)(2,1)} copy(bf16[1,192,1536]{2,1,0:T(8,128)(2,1)} %bitcast.18) | data formatting | bytes 1179648
  144.3 1.9 %copy.16 = bf16[1,192,1536]{2,1,0:T(8,128)(2,1)} copy(bf16[1,192,1536]{2,1,0:T(8,128)(2,1)} %bitcast.17) | data formatting | bytes 1179648
  146.3 1.9 %copy.17 = bf16[1,192,1536]{2,1,0:T(8,128)(2,1)} copy(bf16[1,192,1536]{2,1,0:T(8,128)(2,1)} %bitcast.16) | data formatting | bytes 1179648
  148.2 0.0 copy-done.1
  148.2 1.4 copy.18
  (3 shorter events, 0.0 us)
Async XLA Ops:
  0.6 0.7 copy-start
  142.3 5.9 %copy-start.1 = (bf16[384,3072]{1,0:T(8,128)(2,1)S(1)}, bf16[384,3072]{1,0:T(8,128)(2,1)}, u32[]{:S(2)}) copy-start(bf16[384,3072]{1,0:T(8,128)(2,1)} %get-tuple-element.39) | copy-start | bytes 7077892

commit v3 on v2

--- a/solution.py
+++ b/solution.py
@@ -169,7 +169,7 @@
             pltpu.SemaphoreType.DMA((heads, 2, 2)),
         ],
         compiler_params=pltpu.CompilerParams(
-            collective_id=0, has_side_effects=True, vmem_limit_bytes=VMEM_LIMIT),
+            collective_id=0, has_side_effects=True, vmem_limit_bytes=24 * 1024 * 1024),
         name="gather_heads",
     )(q, k, v, og, ow)
 
@@ -232,7 +232,7 @@
         def back(slot, keys):
             low = p_buf[slot]
             dp = lax.dot_general(gp, vw[0, keys, :], nt, preferred_element_type=jnp.float32)
-            ds = (low.astype(jnp.float32) * (dp - delta)).astype(jnp.bfloat16)
+            ds = low * (dp - delta).astype(jnp.bfloat16)
             dv_buf[keys, :] += lax.dot_general(low, gp, tn, preferred_element_type=jnp.float32)
             dk_buf[keys, :] += lax.dot_general(ds, q[0, rows, :], tn, preferred_element_type=jnp.float32)
             dq_buf[...] += jnp.dot(ds, kw[0, keys, :], preferred_element_type=jnp.float32)
@@ -543,7 +543,7 @@
             pltpu.SemaphoreType.DMA((heads,)),
         ],
         compiler_params=pltpu.CompilerParams(
-            collective_id=1, has_side_effects=True, vmem_limit_bytes=VMEM_LIMIT),
+            collective_id=1, has_side_effects=True, vmem_limit_bytes=24 * 1024 * 1024),
         name="scatter_tokens",
     )(dqh, own, edge, wpart)
 

time: 151 us -> 156 us (1.033); the launches traced: 150 us -> 153 us
  local copies, waits for them, and re-layouts: 7.99 us -> 22 us
  Pallas kernels: 140 us -> 129 us
    unnamed x8 -> x32, local copies, waits for them, and re-layouts: 7.32 us -> 21.2 us
    pallas_call x1, Pallas kernels: 64.5 us -> 52 us  [scatter_tokens(): pl.pallas_call(functools.partial(out_kernel, n_dp, n_uly, n_ctx, heads),...]
    pallas_call x1, Pallas kernels: 29.6 us -> 31.8 us  [attend(): pl.pallas_call(attend_kernel, out_shape=(jax.ShapeDtypeStruct((heads, LAY...]
where the time goes in v3:
time: 156 us; the launch traced here: 153 us
  Pallas kernels  129 us (83%)
  local copies, waits for them, and re-layouts  22 us (14%)
    pallas_call x1, Pallas kernels, scatter_tokens(): pl.pallas_call(functools.partial(out_kernel, n_dp, n_uly, n_ctx, heads),...  52 us
    pallas_call x1, Pallas kernels, gather_heads(): pl.pallas_call(functools.partial(in_kernel, n_uly, n_ctx, heads), out_sha...  45.4 us
    pallas_call x1, Pallas kernels, attend(): pl.pallas_call(attend_kernel, out_shape=(jax.ShapeDtypeStruct((heads, LAY...  31.8 us
    unnamed x32, local copies, waits for them, and re-layouts  21.2 us

profile of v3, /device:TPU:0, one launch (start us, length us, event | category | flops | bytes accessed | tf_op | source)
XLA Modules:
  0.0 152.7 jit_solution(16859688588232708957)
XLA Ops:
  0.6 0.0 copy-start
  0.7 0.7 dynamic-slice_compare_fusion
  1.4 0.0 copy-done
  1.4 0.1 constant_dynamic-slice_fusion
  1.4 0.1 broadcast_compare_fusion
  1.5 0.1 and_convert_fusion
  1.6 0.7 reshape.95.allow
  2.2 0.0 copy-start.1
  2.3 2.3 %copy-done.1 = bf16[1,768,3072]{2,1,0:T(8,128)(2,1)S(1)} copy-done((bf16[1,768,3072]{2,1,0:T(8,128)(2,1)S(1)}, bf16[1,768,3072]{2,1,0:T(8,128)(2,1)}, u32[]{:S(2)}) %copy-start.1) | copy-done | bytes 4718616
  4.6 0.0 copy-start.2
  4.6 1.7 %copy-done.2 = bf16[384,3072]{1,0:T(8,128)(2,1)S(1)} copy-done((bf16[384,3072]{1,0:T(8,128)(2,1)S(1)}, bf16[384,3072]{1,0:T(8,128)(2,1)}, u32[]{:S(2)}) %copy-start.2) | copy-done | bytes 2359320
  6.3 0.0 copy-start.8
  6.3 1.1 copy-done.8
  7.3 0.0 copy-start.9
  7.3 1.1 copy-done.9
  8.4 0.0 copy-start.10
  8.4 1.1 copy-done.10
  9.4 45.4 %gather_heads.1 = (bf16[3,768,128]{2,1,0:T(8,128)(2,1)S(1)}, bf16[3,2304,128]{2,1,0:T(8,128)(2,1)S(1)}, bf16[3,2304,128]{2,1,0:T(8,128)(2,1)S(1)}, bf16[3,768,128]{2,1,0:T(8,128)(2,1)S(1)}) custom-call(bf16[192,1536]{1,0:T(8,128)(2,1)S(1)} %bitcast.13, bf16[192,1536]{1,0:T(8,128)(2,1)S(1)} %bitcast.14, bf16[192,1536]{1,0:T(8,128)(2,1)S(1)} %bitcast.15, ...), custom_call_target="tpu_custom_call" | custom-call | tf_op jit(solution)/shard_map/gather_heads/pallas_call | solution.py:153
  54.8 0.0 copy-start.6
  54.8 1.3 copy-done.6
  56.1 0.0 copy-start.7
  56.1 1.2 copy-done.7
  57.3 0.0 copy-start.11
  57.3 0.8 copy-done.11
  58.1 0.0 copy-start.12
  58.1 0.8 copy-done.12
  59.0 31.8 %attend.1 = (bf16[3,768,128]{2,1,0:T(8,128)(2,1)}, f32[3,2,768,128]{3,2,1,0:T(8,128)}, bf16[3,2,2,768,128]{4,3,2,1,0:T(8,128)(2,1)}, bf16[384,3072]{1,0:T(8,128)(2,1)}) custom-call(s32[36]{0:T(128)} %reshape.95.allow, bf16[3,768,128]{2,1,0:T(8,128)(2,1)} %copy-done.11, bf16[3,2304,128]{2,1,0:T(8,128)(2,1)} %copy-done.6, bf16[3,2304,128]{2,1,0:T(8,128)(2,1)} %copy-done.7, ...), custom_call_target="tpu_custom_call" | custom-call | tf_op jit(solution)/shard_map/attend/pallas_call | solution.py:285
  90.7 0.0 copy-start.3
  90.7 1.7 %copy-done.3 = f32[3,2,768,128]{3,2,1,0:T(8,128)S(1)} copy-done((f32[3,2,768,128]{3,2,1,0:T(8,128)S(1)}, f32[3,2,768,128]{3,2,1,0:T(8,128)}, u32[]{:S(2)}) %copy-start.3) | copy-done | bytes 2359320
  92.4 0.0 copy-start.4
  92.4 1.7 %copy-done.4 = bf16[3,2,2,768,128]{4,3,2,1,0:T(8,128)(2,1)S(1)} copy-done((bf16[3,2,2,768,128]{4,3,2,1,0:T(8,128)(2,1)S(1)}, bf16[3,2,2,768,128]{4,3,2,1,0:T(8,128)(2,1)}, u32[]{:S(2)}) %copy-start.4) | copy-done | bytes 2359320
  94.1 0.0 copy-start.5
  94.1 1.7 %copy-done.5 = bf16[384,3072]{1,0:T(8,128)(2,1)S(1)} copy-done((bf16[384,3072]{1,0:T(8,128)(2,1)S(1)}, bf16[384,3072]{1,0:T(8,128)(2,1)}, u32[]{:S(2)}) %copy-start.5) | copy-done | bytes 2359320
  95.7 0.0 copy-start.13
  95.7 1.1 copy-done.13
  96.8 52.0 %scatter_tokens.1 = (bf16[192,1536]{1,0:T(8,128)(2,1)S(1)}, bf16[192,1536]{1,0:T(8,128)(2,1)S(1)}, bf16[192,1536]{1,0:T(8,128)(2,1)S(1)}, bf16[384,3072]{1,0:T(8,128)(2,1)S(1)}) custom-call(bf16[3,768,128]{2,1,0:T(8,128)(2,1)S(1)} %copy-done.13, f32[3,2,768,128]{3,2,1,0:T(8,128)S(1)} %copy-done.3, bf16[3,2,2,768,128]{4,3,2,1,0:T(8,128)(2,1)S(1)} %copy-done.4, ...), custom_call_target="tpu_custom_call" | custom-call | tf_op jit(solution)/shard_map/scatter_tokens/pallas_call | solution.py:521
  148.8 0.8 copy.15
  149.6 0.8 copy.16
  150.4 0.8 copy.17
  151.2 1.4 copy.18
  (3 shorter events, 0.0 us)
Async XLA Ops:
  0.6 0.7 copy-start
  2.2 2.3 %copy-start.1 = (bf16[1,768,3072]{2,1,0:T(8,128)(2,1)S(1)}, bf16[1,768,3072]{2,1,0:T(8,128)(2,1)}, u32[]{:S(2)}) copy-start(bf16[1,768,3072]{2,1,0:T(8,128)(2,1)} %param.10) | copy-start | bytes 14155780
  4.6 1.7 %copy-start.2 = (bf16[384,3072]{1,0:T(8,128)(2,1)S(1)}, bf16[384,3072]{1,0:T(8,128)(2,1)}, u32[]{:S(2)}) copy-start(bf16[384,3072]{1,0:T(8,128)(2,1)} %ow.1) | copy-start | bytes 7077892
  6.3 1.1 copy-start.8
  7.3 1.1 copy-start.9
  8.4 1.1 copy-start.10
  54.8 1.3 copy-start.6
  56.1 1.2 copy-start.7
  57.3 0.8 copy-start.11
  58.1 0.8 copy-start.12
  90.7 1.7 %copy-start.3 = (f32[3,2,768,128]{3,2,1,0:T(8,128)S(1)}, f32[3,2,768,128]{3,2,1,0:T(8,128)}, u32[]{:S(2)}) copy-start(f32[3,2,768,128]{3,2,1,0:T(8,128)} %get-tuple-element.21.own) | copy-start | bytes 7077892
  92.4 1.7 %copy-start.4 = (bf16[3,2,2,768,128]{4,3,2,1,0:T(8,128)(2,1)S(1)}, bf16[3,2,2,768,128]{4,3,2,1,0:T(8,128)(2,1)}, u32[]{:S(2)}) copy-start(bf16[3,2,2,768,128]{4,3,2,1,0:T(8,128)(2,1)} %get-tuple-element.22.edge) | copy-start | bytes 7077892
  94.1 1.7 %copy-start.5 = (bf16[384,3072]{1,0:T(8,128)(2,1)S(1)}, bf16[384,3072]{1,0:T(8,128)(2,1)}, u32[]{:S(2)}) copy-start(bf16[384,3072]{1,0:T(8,128)(2,1)} %get-tuple-element.23.wpart) | copy-start | bytes 7077892
  95.7 1.1 copy-start.13
